TPU v7x, 32 devices: a whole 2x2x4 slice. The times are simulated.
32 devices in a mesh: grp: 8 (over y, x, core), blk: 4 (over z).
Axes of the slice: x: 2, y: 2, z: 4, core: 2. Of those that a mesh axis runs over, the one named last changes fastest.
Arguments:
- targets: bfloat16 [4096, 128], P('blk'), may hold values from -6 to 6
- sources: bfloat16 [32768, 128], P(('grp', 'blk')), may hold values from -6 to 6
- panel: bfloat16 [32768, 32], P(('grp', 'blk')), may hold values from -6 to 6
Outputs:
- basis: float32 [4096, 32], P('blk')
All inputs are finite; a program needn't handle non-finite values.
Results may differ from a plain program's by a relative error of at most 0.0003.
Values may be sent and summed in bfloat16 or wider, within the bound.
A program may use at most 64 MiB of HBM per device.

v0:
```python
import math

import jax
import jax.numpy as jnp
from jax import lax
from jax.sharding import PartitionSpec as P

D = 128


def tile_product(tgt, src, pan):
    tgt_norm = jnp.sum(jnp.square(tgt.astype(jnp.float32)), axis=1)
    src_norm = jnp.sum(jnp.square(src.astype(jnp.float32)), axis=1)
    cross = jnp.dot(tgt, src.T, preferred_element_type=jnp.float32)
    dist = tgt_norm[:, None] + src_norm[None, :] - 2.0 * cross
    weight = jnp.exp(-(4.0 / D) * dist)
    return jnp.dot(weight, pan.astype(jnp.float32), precision=lax.Precision.HIGHEST)


def kernel_product(tgt, src, pan):
    tgt_rows = tgt.shape[0]
    src_rows = src.shape[0]
    tgt_step = math.gcd(tgt_rows, 1024)
    src_step = math.gcd(src_rows, 2048)
    src_tiles = src.reshape(src_rows // src_step, src_step, src.shape[1])
    pan_tiles = pan.reshape(src_rows // src_step, src_step, pan.shape[1])

    def one_block(block):

        def step(total, pieces):
            return (total + tile_product(block, pieces[0], pieces[1]), None)

        start = jnp.zeros((block.shape[0], pan.shape[1]), jnp.float32)
        total, unused = lax.scan(step, start, (src_tiles, pan_tiles))
        return total

    blocks = lax.map(one_block, tgt.reshape(tgt_rows // tgt_step, tgt_step, tgt.shape[1]))
    return blocks.reshape(tgt_rows, pan.shape[1])


def solve_basis(product, lower):
    solved = jax.scipy.linalg.solve_triangular(lower, product.T, lower=True)
    return solved.T


def per_device(targets, sources, panel):
    tgt_rows = targets.shape[0]
    total_rows = tgt_rows * lax.axis_size("blk")
    partial_value = kernel_product(
        targets,
        lax.all_gather(sources, "blk", axis=0, tiled=True),
        lax.all_gather(panel, "blk", axis=0, tiled=True),
    )
    product = lax.psum(partial_value, "grp")
    local_gram = jnp.dot(product.T, product, precision=lax.Precision.HIGHEST)
    gram = lax.psum(local_gram, "blk") / total_rows
    lower = jnp.linalg.cholesky(gram)
    return solve_basis(product, lower)


def solution(mesh):
    in_specs = (P("blk", None), P(("grp", "blk"), None), P(("grp", "blk"), None))
    out_specs = P("blk", None)
    return jax.shard_map(
        per_device, mesh=mesh, in_specs=in_specs, out_specs=out_specs, check_vma=False
    )
```

profile of v0, /device:TPU:0, one launch (start us, length us, event | category | flops | bytes accessed | tf_op | source)
XLA Modules:
  0.0 158.4 jit_solution(2363705711076979274)
XLA Ops:
  6.5 0.0 all-gather.2.cloned.1.call-start
  6.5 0.7 all-gather.2.cloned.1.call-update
  7.3 0.0 all-reduce.2.cloned.1.call-start
  7.3 16.5 %all_gather.7 = bf16[4096,32]{0,1:T(8,128)(2,1)S(1)} all-gather(bf16[1024,32]{0,1:T(8,128)(2,1)} %param.7), channel_id=1, replica_groups=mesh['grp'=8,'blk'=4] {'blk'}, dimensions={0}, use_global_device_ids=true | all-gather | bytes 327680 | tf_op jit(solution)/shard_map/all_gather | solution.py:52
  23.8 0.5 copy.4
  24.3 16.3 %all-gather.2.cloned.1.call-done = bf16[4096,128]{1,0:T(8,128)(2,1)} async-done(((bf16[1024,128]{1,0:T(8,128)(2,1)}), bf16[4096,128]{1,0:T(8,128)(2,1)}) %all-gather.2.cloned.1.call-update) | async-done | bytes 1048592 | tf_op jit(solution)/shard_map/all_gather | solution.py:51
  40.6 29.4 %while.18 = (s32[]{:T(128)}, f32[1024,32]{0,1:T(8,128)S(1)}, bf16[1024,128]{1,0:T(8,128)(2,1)}, bf16[2,2048,128]{2,1,0:T(8,128)(2,1)}, bf16[2,2048,32]{2,1,0:T(8,128)(2,1)S(1)}, /*index=5*/s32[]{:T(128)}, s32[]{:T(128)}) while((s32[]{:T(128)}, f32[1024,32]{0,1:T(8,128)S(1)}, bf16[1024,128]{1,0:T(8,128)(2,1)}, ...), condition=%wide.region_3.4_spmd.clone, body=%wide.region_0.3_spmd.clone.sunk | while | flops 1351808000 | bytes 24404632 | solution.py:34
  40.6 0.0 copy-start
  40.6 0.0 copy-start.1
  40.6 5.7 %fusion.41 = f32[2048,1024]{0,1:T(8,128)} fusion(bf16[1024,128]{1,0:T(8,128)(2,1)} %get-tuple-element.123, bf16[2,2048,128]{2,1,0:T(8,128)(2,1)} %get-tuple-element.124, s32[]{:T(128)} %get-tuple-element.114), kind=kOutput, calls=%fused_computation.13.clone.1 | convolution fusion | flops 536870912 | bytes 9175552 | tf_op jit(solution)/shard_map/while/body/eval_jaxpr/while/body/eval_jaxpr/dot_general | solution.py:14
  46.3 0.0 copy-done
  46.3 0.3 multiply_reduce_fusion.4
  46.6 0.0 copy-done.1
  46.6 0.2 multiply_reduce_fusion.5
  46.8 8.4 %fusion.42 = f32[1024,32]{0,1:T(8,128)S(1)} fusion(f32[2048,1024]{0,1:T(8,128)} %fusion.41, f32[2048]{0:T(1024)S(1)} %multiply_reduce_fusion.4, f32[1024]{0:T(1024)S(1)} %multiply_reduce_fusion.5, bf16[2,2048,32]{2,1,0:T(8,128)(2,1)S(1)} %get-tuple-element.125, s32[]{:T(128)} %get-tuple-element.114, f32[1024,32]{0,1:T(8,128)S(1)} %get-tuple-element.115, ...), kind=kOutput, calls=%fused_computation.10.clone.1 | convolution fusion | flops 813760512 | bytes 9187333 | tf_op jit(solution)/shard_map/while/body/eval_jaxpr/while/body/eval_jaxpr/dot_general | solution.py:17
  55.3 0.0 copy-start
  55.3 0.0 copy-start.1
  55.3 5.7 %fusion.41 = f32[2048,1024]{0,1:T(8,128)} fusion(bf16[1024,128]{1,0:T(8,128)(2,1)} %get-tuple-element.123, bf16[2,2048,128]{2,1,0:T(8,128)(2,1)} %get-tuple-element.124, s32[]{:T(128)} %get-tuple-element.114), kind=kOutput, calls=%fused_computation.13.clone.1 | convolution fusion | flops 536870912 | bytes 9175552 | tf_op jit(solution)/shard_map/while/body/eval_jaxpr/while/body/eval_jaxpr/dot_general | solution.py:14
  61.0 0.0 copy-done
  61.0 0.3 multiply_reduce_fusion.4
  61.3 0.0 copy-done.1
  61.3 0.2 multiply_reduce_fusion.5
  61.6 8.4 %fusion.42 = f32[1024,32]{0,1:T(8,128)S(1)} fusion(f32[2048,1024]{0,1:T(8,128)} %fusion.41, f32[2048]{0:T(1024)S(1)} %multiply_reduce_fusion.4, f32[1024]{0:T(1024)S(1)} %multiply_reduce_fusion.5, bf16[2,2048,32]{2,1,0:T(8,128)(2,1)S(1)} %get-tuple-element.125, s32[]{:T(128)} %get-tuple-element.114, f32[1024,32]{0,1:T(8,128)S(1)} %get-tuple-element.115, ...), kind=kOutput, calls=%fused_computation.10.clone.1 | convolution fusion | flops 813760512 | bytes 9187333 | tf_op jit(solution)/shard_map/while/body/eval_jaxpr/while/body/eval_jaxpr/dot_general | solution.py:17
  70.0 0.0 copy-start.2
  70.0 0.6 copy-done.2
  70.6 0.0 all-reduce.2.cloned.1.call-update
  70.6 52.3 %all-reduce.2.cloned.1.call-done = f32[1024,32]{0,1:T(8,128)} async-done(((f32[1024,32]{0,1:T(8,128)}), f32[1024,32]{0,1:T(8,128)}) %all-reduce.2.cloned.1.call-update) | async-done | bytes 131088 | tf_op jit(solution)/shard_map/psum | solution.py:54
  123.0 1.2 fusion.26
  124.2 18.7 %psum.15 = f32[32,32]{0,1:T(8,128)S(1)} all-reduce(f32[32,32]{0,1:T(8,128)S(1)} %fusion.26), channel_id=1, replica_groups=mesh['grp'=8,'blk'=4] {'blk'}, use_global_device_ids=true, to_apply=%region_5.6 | all-reduce | flops 1024 | bytes 8192 | tf_op jit(solution)/shard_map/psum | solution.py:56
  142.9 0.1 copy.6
  143.0 2.9 %cholesky.16 = f32[32,32]{1,0:T(8,128)S(1)} custom-call(f32[32,32]{1,0:T(8,128)S(1)} %fusion.25), custom_call_target="Cholesky" | custom-call | tf_op jit(solution)/shard_map/jit(cholesky)/cholesky | solution.py:57
  146.0 0.6 compare_reduce_fusion
  146.6 0.7 fusion.22
  147.3 2.4 %custom-call.7 = f32[1,32,32]{1,2,0:T(8,128)S(1)} custom-call(f32[1,32,32]{2,1,0:T(8,128)S(1)} %fusion.22), custom_call_target="InvertDiagBlocksLowerTriangular" | custom-call | tf_op jit(solution)/shard_map/jit(_solve_triangular)/triangular_solve | solution.py:42
  149.7 1.9 %fusion.23 = f32[1024,32]{0,1:T(8,128)} fusion(f32[1024,32]{0,1:T(8,128)} %all-reduce.2.cloned.1.call-done, f32[1,32,32]{1,2,0:T(8,128)S(1)} %custom-call.7), kind=kOutput, calls=%fused_computation.24 | convolution fusion | flops 12582912 | bytes 266240 | tf_op jit(solution)/shard_map/jit(_solve_triangular)/triangular_solve | solution.py:42
  (4 shorter events, 0.0 us)
Async XLA Ops:
  6.5 34.0 %all-gather.2.cloned.1.call-start = ((), (), s32[]{:S(2)}) async-start(), calls=%async_computation | async-start | bytes 1310720 | tf_op jit(solution)/shard_map/all_gather | solution.py:51
  7.3 115.7 %all-reduce.2.cloned.1.call-start = ((), (), s32[]{:S(2)}) async-start(), calls=%async_computation.1 | async-start | bytes 262144 | tf_op jit(solution)/shard_map/psum | solution.py:54
  40.6 5.7 %copy-start = (bf16[2,2048,128]{2,1,0:T(8,128)(2,1)S(1)}, bf16[2,2048,128]{2,1,0:T(8,128)(2,1)}, u32[]{:S(2)}) copy-start(bf16[2,2048,128]{2,1,0:T(8,128)(2,1)} %get-tuple-element.124) | copy-start | bytes 3145732 | tf_op jit(solution)/shard_map/while/body/eval_jaxpr/while
  40.6 6.0 %copy-start.1 = (bf16[1024,128]{1,0:T(8,128)(2,1)S(1)}, bf16[1024,128]{1,0:T(8,128)(2,1)}, u32[]{:S(2)}) copy-start(bf16[1024,128]{1,0:T(8,128)(2,1)} %get-tuple-element.123) | copy-start | bytes 786436 | tf_op jit(solution)/shard_map/while/body/eval_jaxpr/while
  55.3 5.7 %copy-start = (bf16[2,2048,128]{2,1,0:T(8,128)(2,1)S(1)}, bf16[2,2048,128]{2,1,0:T(8,128)(2,1)}, u32[]{:S(2)}) copy-start(bf16[2,2048,128]{2,1,0:T(8,128)(2,1)} %get-tuple-element.124) | copy-start | bytes 3145732 | tf_op jit(solution)/shard_map/while/body/eval_jaxpr/while
  55.3 6.1 %copy-start.1 = (bf16[1024,128]{1,0:T(8,128)(2,1)S(1)}, bf16[1024,128]{1,0:T(8,128)(2,1)}, u32[]{:S(2)}) copy-start(bf16[1024,128]{1,0:T(8,128)(2,1)} %get-tuple-element.123) | copy-start | bytes 786436 | tf_op jit(solution)/shard_map/while/body/eval_jaxpr/while
  70.0 0.7 copy-start.2
Sparse Core Ops, SparseCore 0:
  8.9 31.5 all-gather.1
  70.8 52.1 all-reduce.1
where the time goes:
time: 159 us; the launch traced here: 158 us
  waiting for transfers between devices  69.3 us (44%)
  blocking collectives  35.2 us (22%)
  matrix products  31.3 us (20%)
  between operations  13.5 us (8%)
  other arithmetic  7.8 us (5%)
    psum x1, waiting for transfers between devices, per_device(): product = lax.psum(partial_value, 'grp')  52.3 us
    psum x1, blocking collectives, per_device(): gram = lax.psum(local_gram, 'blk') / total_rows  18.7 us
    dot_general x2, matrix products, tile_product(): jnp.dot(weight, pan.astype(jnp.float32), precision=lax.Precision.HIGHEST)  16.8 us
    all_gather x1, blocking collectives, per_device(): lax.all_gather(panel, 'blk', axis=0, tiled=True)  16.5 us
    all_gather x1, waiting for transfers between devices, per_device(): lax.all_gather(sources, 'blk', axis=0, tiled=True)  16.3 us
    dot_general x2, matrix products, tile_product(): cross = jnp.dot(tgt, src.T, preferred_element_type=jnp.float32)  11.4 us
    another operation x3, other arithmetic, per_device(): lower = jnp.linalg.cholesky(gram)  3.59 us
  transfers between devices with their start and end apart: 2, of which 2 were waited for; matrix products, arithmetic and copies ran while one was open for 0% of the time, Pallas kernels for 0%

commit v1 on v0

v1 whole, which is shorter than its diff:
```python
import functools

import jax
import jax.numpy as jnp
from jax import lax
from jax.experimental import pallas as pl
from jax.experimental.pallas import tpu as pltpu
from jax.sharding import PartitionSpec as P

D = 128
F32 = jnp.float32
BF16 = jnp.bfloat16
HIGHEST = lax.Precision.HIGHEST


def widened(rows, scale, first_own):
    full = rows.astype(F32)
    norm = jnp.sum(full * full, axis=1, keepdims=True) * (-4.0 / D)
    high = norm.astype(BF16).astype(F32)
    rest = norm - high
    mid = rest.astype(BF16).astype(F32)
    low = rest - mid
    lane = lax.broadcasted_iota(jnp.int32, full.shape, 1)
    own = 0 if first_own else 3
    extra = jnp.where(lane < 6, 1.0, 0.0)
    extra = jnp.where(lane == own, high, extra)
    extra = jnp.where(lane == own + 1, mid, extra)
    extra = jnp.where(lane == own + 2, low, extra)
    return jnp.concatenate([(full * scale).astype(BF16), extra.astype(BF16)], axis=1)


def inverse_lower(gram):
    k = gram.shape[0]
    row = lax.broadcasted_iota(jnp.int32, (k, k), 0)
    col = lax.broadcasted_iota(jnp.int32, (k, k), 1)
    left = gram
    right = jnp.where(row == col, 1.0, 0.0).astype(F32)
    for j in range(k - 1):
        inv = 1.0 / left[j : j + 1, j : j + 1]
        factor = jnp.where(row[:, 0:1] > j, left[:, j : j + 1] * inv, 0.0)
        right = right - factor * right[j : j + 1, :]
        left = left - factor * left[j : j + 1, :]
    pivots = jnp.sum(jnp.where(row == col, left, 0.0), axis=1, keepdims=True)
    return right / jnp.sqrt(pivots)


def kernel(
    grp, blk, total_rows,
    tgt, src, pan, out,
    saug, tall, part, rx_core, rx_chip, layer, rx_blk, full, grams,
    tz_s, tz_r, tl_s, tl_r, tc_s, tc_r,
    pc_s, pc_r, pq_s, pq_r, pb_s, pb_r, ag_s, ag_r, gr_s, gr_r,
):
    g = lax.axis_index("grp")
    b = lax.axis_index("blk")
    chips = grp // 2
    c = lax.rem(g, 2)
    q = g // 2
    piece = tgt.shape[0] // grp

    def send(source, dest, ssem, rsem, to_g, to_b):
        return pltpu.make_async_remote_copy(
            src_ref=source, dst_ref=dest, send_sem=ssem, recv_sem=rsem,
            device_id=(to_g, to_b), device_id_type=pl.DeviceIdType.MESH,
        )

    barrier = pltpu.get_barrier_semaphore()
    for f in range(1, grp):
        pl.semaphore_signal(barrier, inc=1, device_id=(lax.rem(g + f, grp), b), device_id_type=pl.DeviceIdType.MESH)
    for d in range(1, blk):
        pl.semaphore_signal(barrier, inc=1, device_id=(g, lax.rem(b + d, blk)), device_id_type=pl.DeviceIdType.MESH)
    pl.semaphore_wait(barrier, grp + blk - 2)

    sent = []

    def go(copy):
        copy.start()
        sent.append(copy)

    def up(d):
        return lax.rem(b + d, blk)

    def down(d):
        return lax.rem(b + blk - d, blk)

    def chip(e):
        return 2 * lax.rem(q + e, chips) + c

    def chip_back(e):
        return 2 * lax.rem(q + chips - e, chips) + c

    sib = 2 * q + 1 - c

    def tz(d):
        rows = tgt.at[pl.ds(pl.multiple_of(g * piece, piece), piece)]
        return send(rows, tall.at[b, g], tz_s.at[d - 1], tz_r.at[d - 1], g, up(d))

    def tl(d, e):
        return send(
            tall.at[down(d), g], tall.at[down(d), g],
            tl_s.at[d - 1, e - 1], tl_r.at[d - 1, e - 1], chip(e), b,
        )

    def tc(d, e):
        where = tall.at[down(d), chip_back(e)]
        return send(where, where, tc_s.at[d - 1, e], tc_r.at[d - 1, e], sib, b)

    for d in range(1, blk):
        go(tz(d))

    saug[...] = widened(src[...], 1.0, False)

    def product(rows):
        taug = widened(rows, 8.0 / D, True)
        power = lax.dot_general(taug, saug[...], (((1,), (1,)), ((), ())), preferred_element_type=F32)
        weight = jnp.exp(power)
        high = weight.astype(BF16)
        low = (weight - high.astype(F32)).astype(BF16)
        sums = jnp.dot(high, pan[...], preferred_element_type=F32)
        sums = sums + jnp.dot(low, pan[...], preferred_element_type=F32)
        return sums.T

    def own_chunks(lo, hi):
        def step(i, carry):
            rows = tgt[pl.ds(pl.multiple_of(i * piece, piece), piece)]
            part[b, lax.rem(i, 2), i // 2] = product(rows)
            return carry
        lax.fori_loop(lo, hi, step, 0)

    def other_chunks(d):
        bb = down(d)

        def step(i, carry):
            part[bb, lax.rem(i, 2), i // 2] = product(tall[bb, i])
            return carry
        lax.fori_loop(0, grp, step, 0)

    def pc(d):
        return send(part.at[down(d), 1 - c], rx_core.at[down(d)], pc_s.at[d], pc_r.at[d], sib, b)

    def pq(d, e):
        return send(
            part.at[down(d), c, lax.rem(q + e, chips)], rx_chip.at[down(d), e - 1],
            pq_s.at[d, e - 1], pq_r.at[d, e - 1], chip(e), b,
        )

    def pb(d):
        return send(layer.at[d], rx_blk.at[d - 1], pb_s.at[d - 1], pb_r.at[d - 1], g, down(d))

    def core_stage(d):
        bb = down(d)
        pc(d).wait_recv()
        part[bb, c] = part[bb, c] + rx_core[bb]
        for e in range(1, chips):
            go(pq(d, e))

    def chip_stage(d):
        bb = down(d)
        total = part[bb, c, q]
        for e in range(1, chips):
            pq(d, e).wait_recv()
            total = total + rx_chip[bb, e - 1]
        layer[d] = total
        if d > 0:
            go(pb(d))

    first, second = grp // 4, (grp * 5) // 8
    own_chunks(0, first)
    for d in range(1, blk):
        tz(d).wait_recv()
        go(tc(d, 0))
        for e in range(1, chips):
            go(tl(d, e))
    own_chunks(first, second)
    for d in range(1, blk):
        for e in range(1, chips):
            tl(d, e).wait_recv()
            go(tc(d, e))
    own_chunks(second, grp)
    go(pc(0))
    for d in range(1, blk):
        for e in range(chips):
            tc(d, e).wait_recv()
        other_chunks(d)
        go(pc(d))
        core_stage(d - 1)
        if d >= 2:
            chip_stage(d - 2)
    core_stage(blk - 1)
    if blk >= 2:
        chip_stage(blk - 2)
    chip_stage(blk - 1)
    mine = layer[0]
    for d in range(1, blk):
        pb(d).wait_recv()
        mine = mine + rx_blk[d - 1]
    full[g] = mine

    def ag(f):
        return send(full.at[g], full.at[g], ag_s.at[f - 1], ag_r.at[f - 1], lax.rem(g + f, grp), b)

    for f in range(1, grp):
        go(ag(f))
    for f in range(1, grp):
        ag(f).wait_recv()

    gram = jnp.zeros(grams.shape[1:], F32)
    for i in range(grp):
        gram = gram + lax.dot_general(
            full[i], full[i], (((1,), (1,)), ((), ())), precision=HIGHEST, preferred_element_type=F32
        )
    grams[b] = gram

    def gr(d):
        return send(grams.at[b], grams.at[b], gr_s.at[d - 1], gr_r.at[d - 1], g, up(d))

    for d in range(1, blk):
        go(gr(d))
    for d in range(1, blk):
        gr(d).wait_recv()
    gram = grams[0]
    for i in range(1, blk):
        gram = gram + grams[i]
    inverse = inverse_lower(gram * (1.0 / total_rows))
    for i in range(grp):
        out[:, i * piece : (i + 1) * piece] = jnp.dot(
            inverse, full[i], precision=HIGHEST, preferred_element_type=F32
        )
    for copy in sent:
        copy.wait_send()


def per_device(grp, blk, targets, sources, panel):
    rows, k = targets.shape[0], panel.shape[1]
    piece = rows // grp
    chips = grp // 2
    dma = lambda *shape: pltpu.SemaphoreType.DMA(shape)
    result = pl.pallas_call(
        functools.partial(kernel, grp, blk, rows * blk),
        out_shape=jax.ShapeDtypeStruct((k, rows), F32),
        in_specs=[pl.BlockSpec(memory_space=pltpu.VMEM)] * 3,
        out_specs=pl.BlockSpec(memory_space=pltpu.VMEM),
        scratch_shapes=[
            pltpu.VMEM((sources.shape[0], 2 * D), BF16),
            pltpu.VMEM((blk, grp, piece, D), BF16),
            pltpu.VMEM((blk, 2, chips, k, piece), F32),
            pltpu.VMEM((blk, chips, k, piece), F32),
            pltpu.VMEM((blk, chips - 1, k, piece), F32),
            pltpu.VMEM((blk, k, piece), F32),
            pltpu.VMEM((blk - 1, k, piece), F32),
            pltpu.VMEM((grp, k, piece), F32),
            pltpu.VMEM((blk, k, k), F32),
            dma(blk - 1), dma(blk - 1),
            dma(blk - 1, chips - 1), dma(blk - 1, chips - 1),
            dma(blk - 1, chips), dma(blk - 1, chips),
            dma(blk), dma(blk),
            dma(blk, chips - 1), dma(blk, chips - 1),
            dma(blk - 1), dma(blk - 1),
            dma(grp - 1), dma(grp - 1),
            dma(blk - 1), dma(blk - 1),
        ],
        compiler_params=pltpu.CompilerParams(
            collective_id=0, has_side_effects=True, vmem_limit_bytes=40 * 1024 * 1024
        ),
    )(targets, sources, panel)
    return result.T


def solution(mesh):
    in_specs = (P("blk", None), P(("grp", "blk"), None), P(("grp", "blk"), None))
    out_specs = P("blk", None)
    return jax.shard_map(
        functools.partial(per_device, mesh.shape["grp"], mesh.shape["blk"]),
        mesh=mesh, in_specs=in_specs, out_specs=out_specs, check_vma=False,
    )
```

time: 159 us -> 51.8 us (0.33)
  waiting for transfers between devices: 69.3 us -> 0 us
  Pallas kernels: 0 us -> 48.9 us
  blocking collectives: 35.2 us -> 0 us
  matrix products: 31.3 us -> 0 us
  between operations: 13.5 us -> 0.03 us
  other arithmetic: 7.8 us -> 0 us
    psum x1 -> x0, waiting for transfers between devices: 52.3 us -> none  [per_device(): product = lax.psum(partial_value, 'grp')]
    pallas_call x0 -> x1, Pallas kernels: none -> 48.9 us  [per_device(): pl.pallas_call(functools.partial(kernel, grp, blk, rows * blk), out_shape...]
    dot_general x5 -> x0, matrix products: 29.4 us -> none  [the longest x2 16.8 us: tile_product(): jnp.dot(weight, pan.astype(jnp.float32), precision=lax.Precision.HIGHEST)]
    psum x1 -> x0, blocking collectives: 18.7 us -> none  [per_device(): gram = lax.psum(local_gram, 'blk') / total_rows]
    all_gather x1 -> x0, blocking collectives: 16.5 us -> none  [per_device(): lax.all_gather(panel, 'blk', axis=0, tiled=True)]
    all_gather x1 -> x0, waiting for transfers between devices: 16.3 us -> none  [per_device(): lax.all_gather(sources, 'blk', axis=0, tiled=True)]
    another operation x5 -> x0, other arithmetic: 6.68 us -> none  [the longest x3 3.59 us: per_device(): lower = jnp.linalg.cholesky(gram)]
    unnamed x2 -> x6, local copies, waits for them, and re-layouts: 0.65 us -> 2.66 us
  transfers between devices with their start and end apart: 2 -> 0, of which waited for: 2 -> 0; matrix products, arithmetic and copies ran while one was open for 0% -> 0% of each run, Pallas kernels for 0% -> 0%
where the time goes in v1:
time: 51.8 us; the launch traced here: 51.6 us
  Pallas kernels  48.9 us (94%)
  local copies, waits for them, and re-layouts  2.66 us (5%)
    pallas_call x1, Pallas kernels, per_device(): pl.pallas_call(functools.partial(kernel, grp, blk, rows * blk), out_shape...  48.9 us
    unnamed x6, local copies, waits for them, and re-layouts  2.66 us

profile of v1, /device:TPU:0, one launch (start us, length us, event | category | flops | bytes accessed | tf_op | source)
XLA Modules:
  0.0 51.6 jit_solution(11607841663761603298)
XLA Ops:
  0.0 0.0 copy-start
  0.0 1.0 %copy.4.pan = bf16[1024,32]{1,0:T(8,128)(2,1)S(1)} copy(bf16[1024,32]{0,1:T(8,128)(2,1)} %param.5) | data formatting | bytes 131072 | tf_op args[2]
  1.1 0.0 copy-done
  1.1 0.0 copy-start.1
  1.1 0.9 %copy-done.1 = bf16[1024,128]{1,0:T(8,128)(2,1)S(1)} copy-done((bf16[1024,128]{1,0:T(8,128)(2,1)S(1)}, bf16[1024,128]{1,0:T(8,128)(2,1)}, u32[]{:S(2)}) %copy-start.1) | copy-done | bytes 262168
  2.0 48.9 %shard_map.37 = f32[32,1024]{1,0:T(8,128)S(1)} custom-call(bf16[1024,128]{1,0:T(8,128)(2,1)S(1)} %copy-done, bf16[1024,128]{1,0:T(8,128)(2,1)S(1)} %copy-done.1, bf16[1024,32]{1,0:T(8,128)(2,1)S(1)} %copy.4.pan), custom_call_target="tpu_custom_call" | custom-call | tf_op jit(solution)/shard_map/pallas_call | solution.py:238
  51.0 0.7 %copy.6 = f32[1024,32]{0,1:T(8,128)} copy(f32[1024,32]{0,1:T(8,128)S(1)} %bitcast.1) | data formatting | bytes 262144
Async XLA Ops:
  0.0 1.1 %copy-start = (bf16[1024,128]{1,0:T(8,128)(2,1)S(1)}, bf16[1024,128]{1,0:T(8,128)(2,1)}, u32[]{:S(2)}) copy-start(bf16[1024,128]{1,0:T(8,128)(2,1)} %tgt.1) | copy-start | bytes 786436
  1.1 1.0 %copy-start.1 = (bf16[1024,128]{1,0:T(8,128)(2,1)S(1)}, bf16[1024,128]{1,0:T(8,128)(2,1)}, u32[]{:S(2)}) copy-start(bf16[1024,128]{1,0:T(8,128)(2,1)} %src.1) | copy-start | bytes 786436

commit v2 on v0

v2 whole, which is shorter than its diff:
```python
import functools

import jax
import jax.numpy as jnp
from jax import lax
from jax.experimental import pallas as pl
from jax.experimental.pallas import tpu as pltpu
from jax.sharding import PartitionSpec as P

D = 128
F32 = jnp.float32
BF16 = jnp.bfloat16
HIGHEST = lax.Precision.HIGHEST


def widened(rows, scale, first_own):
    full = rows.astype(F32)
    norm = jnp.sum(full * full, axis=1, keepdims=True) * (-4.0 / D)
    high = norm.astype(BF16).astype(F32)
    rest = norm - high
    mid = rest.astype(BF16).astype(F32)
    low = rest - mid
    lane = lax.broadcasted_iota(jnp.int32, full.shape, 1)
    own = 0 if first_own else 3
    extra = jnp.where(lane < 6, 1.0, 0.0)
    extra = jnp.where(lane == own, high, extra)
    extra = jnp.where(lane == own + 1, mid, extra)
    extra = jnp.where(lane == own + 2, low, extra)
    return jnp.concatenate([(full * scale).astype(BF16), extra.astype(BF16)], axis=1)


def inverse_lower(gram):
    k = gram.shape[0]
    row = lax.broadcasted_iota(jnp.int32, (k, k), 0)
    col = lax.broadcasted_iota(jnp.int32, (k, k), 1)
    left = gram
    right = jnp.where(row == col, 1.0, 0.0).astype(F32)
    for j in range(k - 1):
        inv = 1.0 / left[j : j + 1, j : j + 1]
        factor = jnp.where(row[:, 0:1] > j, left[:, j : j + 1] * inv, 0.0)
        right = right - factor * right[j : j + 1, :]
        left = left - factor * left[j : j + 1, :]
    pivots = jnp.sum(jnp.where(row == col, left, 0.0), axis=1, keepdims=True)
    return right / jnp.sqrt(pivots)


def kernel(
    grp, blk, total_rows,
    tgt_hbm, src_hbm, pan_hbm, out,
    src, pan, saug, tall, part, rx_rs, layer, rx_z, full,
    in_sem, tz_s, tz_r, tl_s, tl_r, tc_s, tc_r, rs_s, rs_r, zz_s, zz_r, ag_s, ag_r,
):
    g = lax.axis_index("grp")
    b = lax.axis_index("blk")
    chips = grp // 2
    c = lax.rem(g, 2)
    q = g // 2
    sib = 2 * q + 1 - c
    rows = tall.shape[1]
    piece = rows // grp
    k = pan.shape[0]

    def up(d):
        return lax.rem(b + d, blk)

    def down(d):
        return lax.rem(b + blk - d, blk)

    def peer(f):
        return lax.rem(g + f, grp)

    def chip(e):
        return 2 * lax.rem(q + e, chips) + c

    def chip_back(e):
        return 2 * lax.rem(q + chips - e, chips) + c

    def span(i):
        return pl.ds(pl.multiple_of(i * piece, piece), piece)

    barrier = pltpu.get_barrier_semaphore()
    for f in range(1, grp):
        pl.semaphore_signal(barrier, inc=1, device_id=(peer(f), b), device_id_type=pl.DeviceIdType.MESH)
    for d in range(1, blk):
        pl.semaphore_signal(barrier, inc=1, device_id=(g, up(d)), device_id_type=pl.DeviceIdType.MESH)
    load_src = pltpu.make_async_copy(src_hbm, src, in_sem.at[0])
    load_tgt = pltpu.make_async_copy(tgt_hbm, tall.at[b], in_sem.at[1])
    load_pan = pltpu.make_async_copy(pan_hbm, pan, in_sem.at[2])
    load_src.start()
    load_tgt.start()
    load_pan.start()

    def send(source, dest, ssem, rsem, to_g, to_b):
        return pltpu.make_async_remote_copy(
            src_ref=source, dst_ref=dest, send_sem=ssem, recv_sem=rsem,
            device_id=(to_g, to_b), device_id_type=pl.DeviceIdType.MESH,
        )

    def tz(d):
        return send(
            tgt_hbm.at[span(g)], tall.at[b, span(g)], tz_s.at[d - 1], tz_r.at[d - 1], g, up(d)
        )

    def tl(d, e):
        where = tall.at[down(d), span(g)]
        return send(where, where, tl_s.at[d - 1, e - 1], tl_r.at[d - 1, e - 1], chip(e), b)

    def tc(d, e):
        where = tall.at[down(d), span(chip_back(e))]
        return send(where, where, tc_s.at[d - 1, e], tc_r.at[d - 1, e], sib, b)

    def rs(d, f):
        return send(
            part.at[down(d), peer(f)], rx_rs.at[down(d), f - 1],
            rs_s.at[d, f - 1], rs_r.at[d, f - 1], peer(f), b,
        )

    def zz(i, h):
        return send(
            layer.at[i], rx_z.at[i, h - 1], zz_s.at[i, h - 1], zz_r.at[i, h - 1], g, up(h)
        )

    def ag(f):
        return send(full.at[g], full.at[g], ag_s.at[f - 1], ag_r.at[f - 1], peer(f), b)

    load_src.wait()
    saug[...] = widened(src[...], 1.0, False)
    pl.semaphore_wait(barrier, grp + blk - 2)
    for d in range(1, blk):
        tz(d).start()
    load_pan.wait()
    load_tgt.wait()

    def product(bb, start, count):
        taug = widened(tall[bb, start : start + count], 8.0 / D, True)
        step = min(saug.shape[0], 512)
        sums = jnp.zeros((k, count), F32)
        for lo in range(0, saug.shape[0], step):
            power = lax.dot_general(
                saug[lo : lo + step], taug, (((1,), (1,)), ((), ())), preferred_element_type=F32
            )
            weight = jnp.exp(power)
            high = weight.astype(BF16)
            low = (weight - high.astype(F32)).astype(BF16)
            sums = sums + jnp.dot(pan[:, lo : lo + step], high, preferred_element_type=F32)
            sums = sums + jnp.dot(pan[:, lo : lo + step], low, preferred_element_type=F32)
        for i in range(count // piece):
            part[bb, start // piece + i] = sums[:, i * piece : (i + 1) * piece]

    def layer_stage(d):
        i = down(d)
        total = part[i, g]
        for f in range(1, grp):
            rs(d, f).wait_recv()
            total = total + rx_rs[i, f - 1]
        layer[i] = total
        for h in range(1, blk):
            zz(i, h).start()

    product(b, 0, rows // 2)
    for d in range(1, blk):
        tz(d).wait_recv()
        for e in range(1, chips):
            tl(d, e).start()
        tc(d, 0).start()
    product(b, rows // 2, rows // 2)
    for f in range(1, grp):
        rs(0, f).start()
    for d in range(1, blk):
        for e in range(1, chips):
            tl(d, e).wait_recv()
            tc(d, e).start()

    def other(d, carry):
        for e in range(chips):
            tc(d, e).wait_recv()
        product(down(d), 0, rows)
        for f in range(1, grp):
            rs(d, f).start()
        layer_stage(d - 1)
        return carry

    lax.fori_loop(1, blk, other, 0)
    layer_stage(blk - 1)

    gram = jnp.zeros((k, k), F32)
    for i in range(blk):
        total = layer[i]
        for h in range(1, blk):
            zz(i, h).wait_recv()
            total = total + rx_z[i, h - 1]
        layer_done = total
        gram = gram + lax.dot_general(
            layer_done, layer_done, (((1,), (1,)), ((), ())),
            precision=HIGHEST, preferred_element_type=F32,
        )

        @pl.when(b == i)
        def _():
            full[g, 0:k] = layer_done

    if piece > k:
        gram = jnp.concatenate([gram, jnp.zeros((k, piece - k), F32)], axis=1)
    full[g, k : 2 * k] = gram
    for f in range(1, grp):
        ag(f).start()
    for f in range(1, grp):
        ag(f).wait_recv()
    gram = full[0, k : 2 * k, 0:k]
    for i in range(1, grp):
        gram = gram + full[i, k : 2 * k, 0:k]
    inverse = inverse_lower(gram * (1.0 / total_rows))
    for i in range(grp):
        out[:, i * piece : (i + 1) * piece] = jnp.dot(
            inverse, full[i, 0:k], precision=HIGHEST, preferred_element_type=F32
        )
    for d in range(1, blk):
        tz(d).wait_send()
        for e in range(chips):
            tc(d, e).wait_send()
        for e in range(1, chips):
            tl(d, e).wait_send()
    for d in range(blk):
        for f in range(1, grp):
            rs(d, f).wait_send()
        for h in range(1, blk):
            zz(d, h).wait_send()
    for f in range(1, grp):
        ag(f).wait_send()


def per_device(grp, blk, targets, sources, panel):
    rows, k = targets.shape[0], panel.shape[1]
    piece = rows // grp
    chips = grp // 2
    dma = lambda *shape: pltpu.SemaphoreType.DMA(shape)
    result = pl.pallas_call(
        functools.partial(kernel, grp, blk, rows * blk),
        out_shape=jax.ShapeDtypeStruct((k, rows), F32),
        in_specs=[pl.BlockSpec(memory_space=pltpu.HBM)] * 3,
        out_specs=pl.BlockSpec(memory_space=pltpu.VMEM),
        scratch_shapes=[
            pltpu.VMEM(sources.shape, BF16),
            pltpu.VMEM((k, sources.shape[0]), BF16),
            pltpu.VMEM((sources.shape[0], 2 * D), BF16),
            pltpu.VMEM((blk, rows, D), BF16),
            pltpu.VMEM((blk, grp, k, piece), F32),
            pltpu.VMEM((blk, grp - 1, k, piece), F32),
            pltpu.VMEM((blk, k, piece), F32),
            pltpu.VMEM((blk, blk - 1, k, piece), F32),
            pltpu.VMEM((grp, 2 * k, piece), F32),
            dma(3),
            dma(blk - 1), dma(blk - 1),
            dma(blk - 1, chips - 1), dma(blk - 1, chips - 1),
            dma(blk - 1, chips), dma(blk - 1, chips),
            dma(blk, grp - 1), dma(blk, grp - 1),
            dma(blk, blk - 1), dma(blk, blk - 1),
            dma(grp - 1), dma(grp - 1),
        ],
        compiler_params=pltpu.CompilerParams(
            collective_id=0, has_side_effects=True, vmem_limit_bytes=48 * 1024 * 1024
        ),
    )(targets, sources, panel.T)
    return result.T


def solution(mesh):
    in_specs = (P("blk", None), P(("grp", "blk"), None), P(("grp", "blk"), None))
    out_specs = P("blk", None)
    return jax.shard_map(
        functools.partial(per_device, mesh.shape["grp"], mesh.shape["blk"]),
        mesh=mesh, in_specs=in_specs, out_specs=out_specs, check_vma=False,
    )
```

time: 159 us -> 42 us (0.26)
  waiting for transfers between devices: 69.3 us -> 0 us
  Pallas kernels: 0 us -> 38.4 us
  blocking collectives: 35.2 us -> 0 us
  matrix products: 31.3 us -> 0 us
  between operations: 13.5 us -> 0.01 us
  other arithmetic: 7.8 us -> 0 us
  local copies, waits for them, and re-layouts: 1.22 us -> 3.4 us
    psum x1 -> x0, waiting for transfers between devices: 52.3 us -> none  [per_device(): product = lax.psum(partial_value, 'grp')]
    pallas_call x0 -> x1, Pallas kernels: none -> 38.4 us  [per_device(): pl.pallas_call(functools.partial(kernel, grp, blk, rows * blk), out_shape...]
    dot_general x5 -> x0, matrix products: 29.4 us -> none  [the longest x2 16.8 us: tile_product(): jnp.dot(weight, pan.astype(jnp.float32), precision=lax.Precision.HIGHEST)]
    psum x1 -> x0, blocking collectives: 18.7 us -> none  [per_device(): gram = lax.psum(local_gram, 'blk') / total_rows]
    all_gather x1 -> x0, blocking collectives: 16.5 us -> none  [per_device(): lax.all_gather(panel, 'blk', axis=0, tiled=True)]
    all_gather x1 -> x0, waiting for transfers between devices: 16.3 us -> none  [per_device(): lax.all_gather(sources, 'blk', axis=0, tiled=True)]
    another operation x5 -> x0, other arithmetic: 6.68 us -> none  [the longest x3 3.59 us: per_device(): lower = jnp.linalg.cholesky(gram)]
    unnamed x2 -> x7, local copies, waits for them, and re-layouts: 0.65 us -> 3.4 us
  transfers between devices with their start and end apart: 2 -> 0, of which waited for: 2 -> 0; matrix products, arithmetic and copies ran while one was open for 0% -> 0% of each run, Pallas kernels for 0% -> 0%
where the time goes in v2:
time: 42 us; the launch traced here: 41.8 us
  Pallas kernels  38.4 us (91%)
  local copies, waits for them, and re-layouts  3.4 us (8%)
    pallas_call x1, Pallas kernels, per_device(): pl.pallas_call(functools.partial(kernel, grp, blk, rows * blk), out_shape...  38.4 us
    unnamed x7, local copies, waits for them, and re-layouts  3.4 us

profile of v2, /device:TPU:0, one launch (start us, length us, event | category | flops | bytes accessed | tf_op | source)
XLA Modules:
  0.0 41.8 jit_solution(1699428258093818478)
XLA Ops:
  0.0 0.0 copy-start
  0.0 0.9 %copy-done = bf16[1024,128]{1,0:T(8,128)(2,1)S(1)} copy-done((bf16[1024,128]{1,0:T(8,128)(2,1)S(1)}, bf16[1024,128]{1,0:T(8,128)(2,1)}, u32[]{:S(2)}) %copy-start) | copy-done | bytes 262168
  1.0 0.0 copy-start.1
  1.0 0.9 %copy-done.1 = bf16[1024,128]{1,0:T(8,128)(2,1)S(1)} copy-done((bf16[1024,128]{1,0:T(8,128)(2,1)S(1)}, bf16[1024,128]{1,0:T(8,128)(2,1)}, u32[]{:S(2)}) %copy-start.1) | copy-done | bytes 262168
  1.9 0.0 copy-start.2
  1.9 0.8 %copy-done.2 = bf16[1024,32]{0,1:T(8,128)(2,1)S(1)} copy-done((bf16[1024,32]{0,1:T(8,128)(2,1)S(1)}, bf16[1024,32]{0,1:T(8,128)(2,1)}, u32[]{:S(2)}) %copy-start.2) | copy-done | bytes 65560
  2.7 38.4 %shard_map.37 = f32[32,1024]{1,0:T(8,128)S(1)} custom-call(bf16[1024,128]{1,0:T(8,128)(2,1)S(1)} %copy-done, bf16[1024,128]{1,0:T(8,128)(2,1)S(1)} %copy-done.1, bf16[32,1024]{1,0:T(8,128)(2,1)S(1)} %bitcast.3), custom_call_target="tpu_custom_call" | custom-call | tf_op jit(solution)/shard_map/pallas_call | solution.py:237
  41.1 0.7 %copy.5 = f32[1024,32]{0,1:T(8,128)} copy(f32[1024,32]{0,1:T(8,128)S(1)} %bitcast.2) | data formatting | bytes 262144
Async XLA Ops:
  0.0 0.9 %copy-start = (bf16[1024,128]{1,0:T(8,128)(2,1)S(1)}, bf16[1024,128]{1,0:T(8,128)(2,1)}, u32[]{:S(2)}) copy-start(bf16[1024,128]{1,0:T(8,128)(2,1)} %tgt_hbm.1) | copy-start | bytes 786436
  1.0 0.9 %copy-start.1 = (bf16[1024,128]{1,0:T(8,128)(2,1)S(1)}, bf16[1024,128]{1,0:T(8,128)(2,1)}, u32[]{:S(2)}) copy-start(bf16[1024,128]{1,0:T(8,128)(2,1)} %src_hbm.1) | copy-start | bytes 786436
  1.9 0.8 %copy-start.2 = (bf16[1024,32]{0,1:T(8,128)(2,1)S(1)}, bf16[1024,32]{0,1:T(8,128)(2,1)}, u32[]{:S(2)}) copy-start(bf16[1024,32]{0,1:T(8,128)(2,1)} %param.5) | copy-start | bytes 196612

commit v3 on v2

--- a/solution.py
+++ b/solution.py
@@ -61,10 +61,17 @@
     k = pan.shape[0]
 
     def up(d):
-        return lax.rem(b + d, blk)
+        if blk & (blk - 1):
+            return lax.rem(b + d, blk)
+        bit, total = 1, 0
+        while bit < blk:
+            mine, flip = lax.rem(b // bit, 2), (d // bit) % 2
+            total = total + bit * (mine + flip - 2 * mine * flip)
+            bit *= 2
+        return total
 
     def down(d):
-        return lax.rem(b + blk - d, blk)
+        return lax.rem(b + blk - d, blk) if blk & (blk - 1) else up(d)
 
     def peer(f):
         return lax.rem(g + f, grp)
@@ -166,14 +173,22 @@
     product(b, rows // 2, rows // 2)
     for f in range(1, grp):
         rs(0, f).start()
-    for d in range(1, blk):
+
+    def forward(d):
         for e in range(1, chips):
             tl(d, e).wait_recv()
             tc(d, e).start()
 
+    forward(1)
+
     def other(d, carry):
         for e in range(chips):
             tc(d, e).wait_recv()
+
+        @pl.when(d < blk - 1)
+        def _():
+            forward(d + 1)
+
         product(down(d), 0, rows)
         for f in range(1, grp):
             rs(d, f).start()
@@ -199,16 +214,18 @@
         def _():
             full[g, 0:k] = layer_done
 
-    if piece > k:
-        gram = jnp.concatenate([gram, jnp.zeros((k, piece - k), F32)], axis=1)
-    full[g, k : 2 * k] = gram
+    some = k * k // piece
+    full[g, k : k + some] = jnp.concatenate(
+        [gram[i * some : (i + 1) * some] for i in range(k // some)], axis=1
+    )
     for f in range(1, grp):
         ag(f).start()
     for f in range(1, grp):
         ag(f).wait_recv()
-    gram = full[0, k : 2 * k, 0:k]
+    gram = full[0, k : k + some]
     for i in range(1, grp):
-        gram = gram + full[i, k : 2 * k, 0:k]
+        gram = gram + full[i, k : k + some]
+    gram = jnp.concatenate([gram[:, i * k : (i + 1) * k] for i in range(k // some)], axis=0)
     inverse = inverse_lower(gram * (1.0 / total_rows))
     for i in range(grp):
         out[:, i * piece : (i + 1) * piece] = jnp.dot(
@@ -248,7 +265,7 @@
             pltpu.VMEM((blk, grp - 1, k, piece), F32),
             pltpu.VMEM((blk, k, piece), F32),
             pltpu.VMEM((blk, blk - 1, k, piece), F32),
-            pltpu.VMEM((grp, 2 * k, piece), F32),
+            pltpu.VMEM((grp, k + k * k // piece, piece), F32),
             dma(3),
             dma(blk - 1), dma(blk - 1),
             dma(blk - 1, chips - 1), dma(blk - 1, chips - 1),
@@ -258,7 +275,7 @@
             dma(grp - 1), dma(grp - 1),
         ],
         compiler_params=pltpu.CompilerParams(
-            collective_id=0, has_side_effects=True, vmem_limit_bytes=48 * 1024 * 1024
+            collective_id=0, has_side_effects=True, vmem_limit_bytes=64 * 1024 * 1024 - 65536
         ),
     )(targets, sources, panel.T)
     return result.T

time: 42 us -> 39.4 us (0.938)
  local copies, waits for them, and re-layouts: 3.4 us -> 1.57 us
  Pallas kernels: 38.4 us -> 37.7 us
    unnamed x7 -> x1, local copies, waits for them, and re-layouts: 3.4 us -> 1.57 us
    pallas_call x1, Pallas kernels: 38.4 us -> 37.7 us  [per_device(): pl.pallas_call(functools.partial(kernel, grp, blk, rows * blk), out_shape...]
where the time goes in v3:
time: 39.4 us; the launch traced here: 39.3 us
  Pallas kernels  37.7 us (96%)
  local copies, waits for them, and re-layouts  1.57 us (4%)
    pallas_call x1, Pallas kernels, per_device(): pl.pallas_call(functools.partial(kernel, grp, blk, rows * blk), out_shape...  37.7 us
    unnamed x1, local copies, waits for them, and re-layouts  1.57 us

profile of v3, /device:TPU:0, one launch (start us, length us, event | category | flops | bytes accessed | tf_op | source)
XLA Modules:
  0.0 39.3 jit_solution(11778301759324904845)
XLA Ops:
  0.0 37.7 %shard_map.37 = f32[32,1024]{1,0:T(8,128)} custom-call(bf16[1024,128]{1,0:T(8,128)(2,1)} %tgt_hbm.1, bf16[1024,128]{1,0:T(8,128)(2,1)} %src_hbm.1, bf16[32,1024]{1,0:T(8,128)(2,1)} %bitcast.3), custom_call_target="tpu_custom_call" | custom-call | tf_op jit(solution)/shard_map/pallas_call | solution.py:254
  37.7 1.6 %copy.5 = f32[1024,32]{0,1:T(8,128)} copy(f32[1024,32]{0,1:T(8,128)} %bitcast.2) | data formatting | bytes 262144

commit v4 on v3

--- a/solution.py
+++ b/solution.py
@@ -1,4 +1,5 @@
 import functools
+import math
 
 import jax
 import jax.numpy as jnp
@@ -35,11 +36,16 @@
     col = lax.broadcasted_iota(jnp.int32, (k, k), 1)
     left = gram
     right = jnp.where(row == col, 1.0, 0.0).astype(F32)
-    for j in range(k - 1):
-        inv = 1.0 / left[j : j + 1, j : j + 1]
-        factor = jnp.where(row[:, 0:1] > j, left[:, j : j + 1] * inv, 0.0)
-        right = right - factor * right[j : j + 1, :]
-        left = left - factor * left[j : j + 1, :]
+    group = math.gcd(k, 8)
+    for start in range(0, k, group):
+        cols = [jnp.broadcast_to(left[:, j : j + 1], (k, k)) for j in range(start, start + group)]
+        for m in range(group):
+            j = start + m
+            factor = jnp.where(row > j, cols[m] * (1.0 / cols[m][j : j + 1, :]), 0.0)
+            right = right - factor * right[j : j + 1, :]
+            left = left - factor * left[j : j + 1, :]
+            for n in range(m + 1, group):
+                cols[n] = cols[n] - factor * cols[n][j : j + 1, :]
     pivots = jnp.sum(jnp.where(row == col, left, 0.0), axis=1, keepdims=True)
     return right / jnp.sqrt(pivots)
 
@@ -164,22 +170,28 @@
         for h in range(1, blk):
             zz(i, h).start()
 
-    product(b, 0, rows // 2)
-    for d in range(1, blk):
+    def share(d):
         tz(d).wait_recv()
         for e in range(1, chips):
             tl(d, e).start()
         tc(d, 0).start()
-    product(b, rows // 2, rows // 2)
-    for f in range(1, grp):
-        rs(0, f).start()
 
     def forward(d):
         for e in range(1, chips):
             tl(d, e).wait_recv()
             tc(d, e).start()
 
+    half = rows // 2
+    share(1)
+    product(b, 0, half)
+    for d in range(2, min(blk, 3)):
+        share(d)
     forward(1)
+    product(b, half, half)
+    for f in range(1, grp):
+        rs(0, f).start()
+    for d in range(3, blk):
+        share(d)
 
     def other(d, carry):
         for e in range(chips):
@@ -275,7 +287,7 @@
             dma(grp - 1), dma(grp - 1),
         ],
         compiler_params=pltpu.CompilerParams(
-            collective_id=0, has_side_effects=True, vmem_limit_bytes=64 * 1024 * 1024 - 65536
+            collective_id=0, has_side_effects=True, vmem_limit_bytes=64 * 1024 * 1024 - 196608
         ),
     )(targets, sources, panel.T)
     return result.T

time: 39.4 us -> 37.8 us (0.959)
  Pallas kernels: 37.7 us -> 36.1 us
    pallas_call x1, Pallas kernels: 37.7 us -> 36.1 us  [per_device(): pl.pallas_call(functools.partial(kernel, grp, blk, rows * blk), out_shape...]
where the time goes in v4:
time: 37.8 us; the launch traced here: 37.7 us
  Pallas kernels  36.1 us (96%)
  local copies, waits for them, and re-layouts  1.57 us (4%)
    pallas_call x1, Pallas kernels, per_device(): pl.pallas_call(functools.partial(kernel, grp, blk, rows * blk), out_shape...  36.1 us
    unnamed x1, local copies, waits for them, and re-layouts  1.57 us

profile of v4, /device:TPU:0, one launch (start us, length us, event | category | flops | bytes accessed | tf_op | source)
XLA Modules:
  0.0 37.7 jit_solution(5664008480493534099)
XLA Ops:
  0.0 36.1 %shard_map.37 = f32[32,1024]{1,0:T(8,128)} custom-call(bf16[1024,128]{1,0:T(8,128)(2,1)} %tgt_hbm.1, bf16[1024,128]{1,0:T(8,128)(2,1)} %src_hbm.1, bf16[32,1024]{1,0:T(8,128)(2,1)} %bitcast.3), custom_call_target="tpu_custom_call" | custom-call | tf_op jit(solution)/shard_map/pallas_call | solution.py:266
  36.1 1.6 %copy.5 = f32[1024,32]{0,1:T(8,128)} copy(f32[1024,32]{0,1:T(8,128)} %bitcast.2) | data formatting | bytes 262144

commit v5 on v4

--- a/solution.py
+++ b/solution.py
@@ -111,7 +111,7 @@
 
     def tz(d):
         return send(
-            tgt_hbm.at[span(g)], tall.at[b, span(g)], tz_s.at[d - 1], tz_r.at[d - 1], g, up(d)
+            tall.at[b, span(g)], tall.at[b, span(g)], tz_s.at[d - 1], tz_r.at[d - 1], g, up(d)
         )
 
     def tl(d, e):
@@ -138,11 +138,11 @@
 
     load_src.wait()
     saug[...] = widened(src[...], 1.0, False)
+    load_tgt.wait()
+    load_pan.wait()
     pl.semaphore_wait(barrier, grp + blk - 2)
     for d in range(1, blk):
         tz(d).start()
-    load_pan.wait()
-    load_tgt.wait()
 
     def product(bb, start, count):
         taug = widened(tall[bb, start : start + count], 8.0 / D, True)
@@ -287,9 +287,9 @@
             dma(grp - 1), dma(grp - 1),
         ],
         compiler_params=pltpu.CompilerParams(
-            collective_id=0, has_side_effects=True, vmem_limit_bytes=64 * 1024 * 1024 - 196608
+            collective_id=0, has_side_effects=True, vmem_limit_bytes=48 * 1024 * 1024
         ),
-    )(targets, sources, panel.T)
+    )(*[pltpu.with_memory_space_constraint(x, pltpu.HBM) for x in (targets, sources, panel.T)])
     return result.T
 
 

time: 37.8 us -> 36 us (0.952)
  local copies, waits for them, and re-layouts: 1.57 us -> 0.66 us
  Pallas kernels: 36.1 us -> 35.2 us
    unnamed x1, local copies, waits for them, and re-layouts: 1.57 us -> 0.66 us
    pallas_call x1, Pallas kernels: 36.1 us -> 35.2 us  [per_device(): pl.pallas_call(functools.partial(kernel, grp, blk, rows * blk), out_shape...]
where the time goes in v5:
time: 36 us; the launch traced here: 35.9 us
  Pallas kernels  35.2 us (98%)
  local copies, waits for them, and re-layouts  0.66 us (2%)
    pallas_call x1, Pallas kernels, per_device(): pl.pallas_call(functools.partial(kernel, grp, blk, rows * blk), out_shape...  35.2 us

profile of v5, /device:TPU:0, one launch (start us, length us, event | category | flops | bytes accessed | tf_op | source)
XLA Modules:
  0.0 35.9 jit_solution(8708570895267255925)
XLA Ops:
  0.0 35.2 %shard_map.37 = f32[32,1024]{1,0:T(8,128)S(1)} custom-call(bf16[1024,128]{1,0:T(8,128)(2,1)} %tgt_hbm.1, bf16[1024,128]{1,0:T(8,128)(2,1)} %src_hbm.1, bf16[32,1024]{1,0:T(8,128)(2,1)} %bitcast.3), custom_call_target="tpu_custom_call" | custom-call | tf_op jit(solution)/shard_map/pallas_call | solution.py:266
  35.2 0.7 %copy.5 = f32[1024,32]{0,1:T(8,128)} copy(f32[1024,32]{0,1:T(8,128)S(1)} %bitcast.2) | data formatting | bytes 262144
